TPU v7x, 256 devices: a whole 4x4x8 slice. The times are simulated.
256 devices in a mesh: seq: 64 (over y, x_hi, z), ch: 4 (over x_lo, core).
Axes of the slice: x: 4 (x_hi: 2, x_lo: 2; x = x_hi * 2 + x_lo), y: 4, z: 8, core: 2. Of those that a mesh axis runs over, the one named last changes fastest.
Arguments:
- streams: bfloat16 [16384, 3, 4096], P(('seq', 'ch')), may hold values from -6 to 6
- filter_taps: float32 [4096, 16384], P('ch', 'seq')
- skip_gain: float32 [4096], P('ch'), may hold values from -1 to 1
Outputs:
- mixed_out: bfloat16 [4096, 16384], P('ch', 'seq')
All inputs are finite; a program needn't handle non-finite values.
Results may differ from a plain program's by a relative error of at most 0.001.
Values may be sent and summed in bfloat16 or wider, within the bound.
A program may use at most 128 MiB of HBM per device.

v0:
```python
import math

import jax
import jax.numpy as jnp
from jax import lax
from jax.sharding import PartitionSpec as P

PRECISE = lax.Precision.HIGHEST


def angles(left_index, right_index, period):
    product = left_index[:, None] * right_index[None, :] % period
    phase_angle = product.astype(jnp.float32) * (2.0 * math.pi / period)
    return (jnp.cos(phase_angle), jnp.sin(phase_angle))


def spectral_product(spec_re, spec_im):
    prod_re = spec_re[0] * spec_re[1] - spec_im[0] * spec_im[1]
    prod_im = spec_re[0] * spec_im[1] + spec_im[0] * spec_re[1]
    return (prod_re, prod_im)


def lanes_forward_blocks(blocks, offset, length_fft):
    block_count = blocks.shape[1]
    row_count = blocks.shape[2]
    j_range = jnp.arange(block_count, dtype=jnp.int32)
    k_range = jnp.arange(2 * block_count, dtype=jnp.int32)
    cos_blocks, sin_blocks = angles(j_range, k_range, 2 * block_count)
    real_part = jnp.einsum("sjmc,jk->skmc", blocks, cos_blocks, precision=PRECISE)
    imag_part = -jnp.einsum("sjmc,jk->skmc", blocks, sin_blocks, precision=PRECISE)
    m_global = offset + jnp.arange(row_count, dtype=jnp.int32)
    cos_twist, sin_twist = angles(k_range, m_global, length_fft)
    cos_twist = cos_twist[:, :, None]
    sin_twist = sin_twist[:, :, None]
    return (
        real_part * cos_twist + imag_part * sin_twist,
        imag_part * cos_twist - real_part * sin_twist,
    )


def lanes_forward_rows(real_part, imag_part):
    row_count = real_part.shape[2]
    indices = jnp.arange(row_count, dtype=jnp.int32)
    cos_rows, sin_rows = angles(indices, indices, row_count)
    spec_re = jnp.einsum("skrc,rq->skqc", real_part, cos_rows, precision=PRECISE) + jnp.einsum(
        "skrc,rq->skqc", imag_part, sin_rows, precision=PRECISE
    )
    spec_im = jnp.einsum("skrc,rq->skqc", imag_part, cos_rows, precision=PRECISE) - jnp.einsum(
        "skrc,rq->skqc", real_part, sin_rows, precision=PRECISE
    )
    return (spec_re, spec_im)


def lanes_inverse_rows(real_part, imag_part, k_global, length_fft):
    row_count = real_part.shape[1]
    indices = jnp.arange(row_count, dtype=jnp.int32)
    cos_rows, sin_rows = angles(indices, indices, row_count)
    back_re = jnp.einsum("kqc,qr->krc", real_part, cos_rows, precision=PRECISE) - jnp.einsum(
        "kqc,qr->krc", imag_part, sin_rows, precision=PRECISE
    )
    back_im = jnp.einsum("kqc,qr->krc", imag_part, cos_rows, precision=PRECISE) + jnp.einsum(
        "kqc,qr->krc", real_part, sin_rows, precision=PRECISE
    )
    cos_twist, sin_twist = angles(k_global, indices, length_fft)
    cos_twist = cos_twist[:, :, None]
    sin_twist = sin_twist[:, :, None]
    return (back_re * cos_twist - back_im * sin_twist, back_im * cos_twist + back_re * sin_twist)


def lanes_inverse_blocks(real_part, imag_part, keep_count, length_fft):
    double_count = real_part.shape[0]
    k_range = jnp.arange(double_count, dtype=jnp.int32)
    j_range = jnp.arange(keep_count, dtype=jnp.int32)
    cos_blocks, sin_blocks = angles(k_range, j_range, double_count)
    summed = jnp.einsum("kmc,kj->jmc", real_part, cos_blocks, precision=PRECISE) - jnp.einsum(
        "kmc,kj->jmc", imag_part, sin_blocks, precision=PRECISE
    )
    return summed * (1.0 / length_fft)


def body(streams, filter_taps, skip_gain):
    local_channels = filter_taps.shape[0]
    regrouped = lax.all_to_all(streams, "ch", split_axis=2, concat_axis=0, tiled=True)
    channel_major = jnp.transpose(regrouped, (2, 1, 0))
    queries = channel_major[:, 0, :].astype(jnp.float32)
    gated_values = channel_major[:, 1, :].astype(jnp.float32) * channel_major[:, 2, :].astype(
        jnp.float32
    )
    tok_count = gated_values.shape[1]
    groups = lax.axis_size("seq")
    length_fft = 2 * tok_count * groups
    block_len = tok_count // groups
    position = lax.axis_index("seq")
    gated_rows = regrouped[:, 1, :].astype(jnp.float32) * regrouped[:, 2, :].astype(jnp.float32)
    stacked_rows = jnp.stack([gated_rows, jnp.transpose(filter_taps)])
    columns = lax.all_to_all(
        stacked_rows.reshape(2, groups, block_len, local_channels),
        "seq",
        split_axis=1,
        concat_axis=1,
        tiled=True,
    )
    real_part, imag_part = lanes_forward_blocks(columns, position * block_len, length_fft)
    exchanged = lax.all_to_all(
        jnp.stack([real_part, imag_part]), "seq", split_axis=2, concat_axis=3, tiled=True
    )
    spec_re, spec_im = lanes_forward_rows(exchanged[0], exchanged[1])
    prod_re, prod_im = spectral_product(spec_re, spec_im)
    local_k = prod_re.shape[0]
    k_global = position * local_k + jnp.arange(local_k, dtype=jnp.int32)
    back_re, back_im = lanes_inverse_rows(prod_re, prod_im, k_global, length_fft)
    returned = lax.all_to_all(
        jnp.stack([back_re, back_im]), "seq", split_axis=2, concat_axis=1, tiled=True
    )
    inverted = lanes_inverse_blocks(returned[0], returned[1], groups, length_fft)
    convolved_rows = lax.all_to_all(
        inverted, "seq", split_axis=0, concat_axis=0, tiled=True
    ).reshape(tok_count, local_channels)
    convolved = jnp.transpose(convolved_rows)
    mixed_sum = convolved + skip_gain[:, None] * gated_values
    return (queries * mixed_sum).astype(jnp.bfloat16)


def solution(mesh):
    placed = (P(("seq", "ch"), None, None), P("ch", "seq"), P("ch"))
    return jax.shard_map(
        body, mesh=mesh, in_specs=placed, out_specs=P("ch", "seq"), check_vma=False
    )
```

profile of v0, /device:TPU:32, one launch (start us, length us, event | category | flops | bytes accessed | tf_op | source)
XLA Modules:
  0.0 570.9 jit_solution(14144552524962424668)
XLA Ops:
  0.0 6.4 %copy.28 = bf16[64,3,4096]{0,1,2:T(4,128)(2,1)} copy(bf16[64,3,4096]{2,0,1:T(8,128)(2,1)} %param.3) | data formatting | bytes 3145728 | tf_op args[0]
  6.4 5.5 reshape.183
  11.9 3.6 all-to-all-start
  15.4 1.6 copy.31
  17.0 2.2 stack.33
  19.3 16.2 %all-to-all-done = bf16[4,2,98304]{2,1,0:T(2,128)(2,1)S(1)} async-done(((bf16[4,2,98304]{2,1,0:T(2,128)(2,1)}), bf16[4,2,98304]{2,1,0:T(2,128)(2,1)S(1)}, u32[]{:S(2)}, u32[]{:S(2)}) %all-to-all-start) | async-done | bytes 1572896 | tf_op jit(solution)/shard_map/all_to_all | solution.py:83
  35.5 3.8 reshape.184
  39.3 5.4 copy.30
  44.7 0.0 copy-start.3
  44.8 0.2 convert_multiply_fusion.1
  44.9 2.2 mul.334
  47.2 0.0 copy-done.3
  47.2 3.6 pad_maximum_fusion.2
  50.8 2.3 copy.33
  53.1 14.4 %all-to-all-start.1 = ((f32[2,64,4,1024]{3,2,0,1:T(4,128)}), f32[2,64,4,1024]{3,2,0,1:T(4,128)S(1)}, u32[]{:S(2)}, u32[]{:S(2)}) async-start(f32[2,64,4,1024]{3,2,0,1:T(4,128)} %copy.33), calls=%async_computation.1 | async-start | bytes 4194304 | tf_op jit(solution)/shard_map/all_to_all | solution.py:96
  67.5 0.1 fusion.85
  67.6 51.5 %all-to-all-done.1 = f32[2,64,4,1024]{3,2,0,1:T(4,128)S(1)} async-done(((f32[2,64,4,1024]{3,2,0,1:T(4,128)}), f32[2,64,4,1024]{3,2,0,1:T(4,128)S(1)}, u32[]{:S(2)}, u32[]{:S(2)}) %all-to-all-start.1) | async-done | bytes 2097184 | tf_op jit(solution)/shard_map/all_to_all | solution.py:96
  119.2 4.6 fusion.12
  123.8 5.7 add_bitcast_fusion.1
  129.5 4.1 pad_maximum_fusion
  133.6 12.4 %copy.36 = f32[2,2,128,4,1024]{4,3,1,0,2:T(4,128)} copy(f32[2,2,128,4,1024]{4,2,3,1,0:T(8,128)} %pad_maximum_fusion) | data formatting | bytes 16777216 | tf_op jit(solution)/shard_map/stack | solution.py:105
  146.0 7.1 %all-to-all-start.2 = ((f32[2,2,128,4,1024]{4,3,1,0,2:T(4,128)}), f32[2,2,128,4,1024]{4,3,1,0,2:T(4,128)}, u32[]{:S(2)}, u32[]{:S(2)}) async-start(f32[2,2,128,4,1024]{4,3,1,0,2:T(4,128)} %copy.36), calls=%async_computation.2 | async-start | bytes 16777216 | tf_op jit(solution)/shard_map/all_to_all | solution.py:104
  153.2 0.1 fusion.83
  153.3 184.5 %all-to-all-done.2 = f32[2,2,128,4,1024]{4,3,1,0,2:T(4,128)} async-done(((f32[2,2,128,4,1024]{4,3,1,0,2:T(4,128)}), f32[2,2,128,4,1024]{4,3,1,0,2:T(4,128)}, u32[]{:S(2)}, u32[]{:S(2)}) %all-to-all-start.2) | async-done | bytes 8388640 | tf_op jit(solution)/shard_map/all_to_all | solution.py:104
  337.8 9.4 %copy.56 = f32[2,2,64,2,4,1024]{5,4,2,3,1,0:T(4,128)} copy(f32[2,2,64,2,4,1024]{5,4,1,0,3,2:T(4,128)} %bitcast.20) | data formatting | bytes 16777216 | tf_op jit(solution)/shard_map/all_to_all | solution.py:104
  347.2 8.9 %fusion.134 = (f32[1,2,2,64,4,1024]{5,4,3,2,1,0:T(4,128)}, f32[1,2,2,64,4,1024]{5,4,3,2,1,0:T(4,128)}) fusion(f32[2,2,2,64,4,1024]{5,4,3,2,1,0:T(4,128)} %bitcast.137), kind=kLoop, calls=%fused_computation.155 | loop fusion | bytes 16777216 | tf_op jit(solution)/shard_map/slice | solution.py:107
  356.1 5.3 squeeze.8
  361.4 9.2 %fusion.34 = f32[256,2,2,1024]{3,0,2,1:T(8,128)} fusion(f32[2,2,256,1024]{3,2,1,0:T(8,128)} %squeeze.8), kind=kOutput, calls=%fused_computation.53 | convolution fusion | flops 3222142976 | bytes 8388608 | tf_op jit(solution)/shard_map/skrc,rq->skqc/dot_general | solution.py:45
  370.5 5.3 squeeze.9
  375.8 0.0 copy-start.1
  375.8 0.0 copy-start.2
  375.8 7.8 %fusion.32 = f32[256,2,2,1024]{3,0,2,1:T(8,128)S(1)} fusion(f32[2,2,256,1024]{3,2,1,0:T(8,128)} %squeeze.9), kind=kOutput, calls=%fused_computation.51 | convolution fusion | flops 3222142976 | bytes 8388608 | tf_op jit(solution)/shard_map/skrc,rq->skqc/dot_general | solution.py:48
  383.6 0.0 copy-done.1
  383.6 0.0 copy-done.2
  383.6 0.0 copy-start
  383.7 5.1 add_bitcast_fusion
  388.8 0.0 copy-done
  388.8 5.1 subtract_bitcast_fusion
  393.9 1.4 multiply_subtract_fusion
  395.4 3.3 fusion.6
  398.7 2.9 fusion.4
  401.6 3.0 fusion.16
  404.5 3.5 fusion.1
  408.0 0.3 pad_maximum_fusion.1
  408.3 3.4 copy.38
  411.7 105.3 %all_to_all.58 = f32[2,2,256,1024]{3,1,0,2:T(2,128)S(1)} all-to-all(f32[2,2,256,1024]{3,1,0,2:T(2,128)S(1)} %copy.38), channel_id=1, replica_groups=mesh['seq'=64,'ch'=4] {'seq'}, dimensions={2} | all-to-all | bytes 8388608 | tf_op jit(solution)/shard_map/all_to_all | solution.py:112
  517.0 1.8 copy.57
  518.8 3.4 fusion.135
  522.2 2.7 squeeze.10
  524.9 1.3 fusion.60
  526.2 2.7 squeeze.11
  528.9 1.3 fusion.22
  530.3 0.7 copy.40
  531.0 0.0 copy-start.4
  531.0 0.0 copy-start.5
  531.0 36.7 %all_to_all.59 = f32[64,4,1024]{2,1,0:T(4,128)} all-to-all(f32[64,4,1024]{2,1,0:T(4,128)S(1)} %copy.40), channel_id=1, replica_groups=mesh['seq'=64,'ch'=4] {'seq'}, dimensions={0} | all-to-all | bytes 2097152 | tf_op jit(solution)/shard_map/all_to_all | solution.py:116
  567.7 1.6 reshape.173
  569.3 0.0 copy-done.4
  569.3 0.0 copy-done.5
  569.4 0.3 fusion.23
  569.7 1.0 copy.41
  (2 shorter events, 0.0 us)
Async XLA Ops:
  11.9 23.6 %all-to-all-start = ((bf16[4,2,98304]{2,1,0:T(2,128)(2,1)}), bf16[4,2,98304]{2,1,0:T(2,128)(2,1)S(1)}, u32[]{:S(2)}, u32[]{:S(2)}) async-start(bf16[4,2,98304]{2,1,0:T(2,128)(2,1)} %reshape.183), calls=%async_computation | async-start | bytes 3145728 | tf_op jit(solution)/shard_map/all_to_all | solution.py:83
  44.7 2.4 copy-start.3
  53.1 66.1 %all-to-all-start.1 = ((f32[2,64,4,1024]{3,2,0,1:T(4,128)}), f32[2,64,4,1024]{3,2,0,1:T(4,128)S(1)}, u32[]{:S(2)}, u32[]{:S(2)}) async-start(f32[2,64,4,1024]{3,2,0,1:T(4,128)} %copy.33), calls=%async_computation.1 | async-start | bytes 4194304 | tf_op jit(solution)/shard_map/all_to_all | solution.py:96
  146.0 191.8 %all-to-all-start.2 = ((f32[2,2,128,4,1024]{4,3,1,0,2:T(4,128)}), f32[2,2,128,4,1024]{4,3,1,0,2:T(4,128)}, u32[]{:S(2)}, u32[]{:S(2)}) async-start(f32[2,2,128,4,1024]{4,3,1,0,2:T(4,128)} %copy.36), calls=%async_computation.2 | async-start | bytes 16777216 | tf_op jit(solution)/shard_map/all_to_all | solution.py:104
  375.8 7.8 %copy-start.1 = (f32[2,2,256,1024]{3,2,1,0:T(8,128)S(1)}, f32[2,2,256,1024]{3,2,1,0:T(8,128)}, u32[]{:S(2)}) copy-start(f32[2,2,256,1024]{3,2,1,0:T(8,128)} %squeeze.9) | copy-start | bytes 12582916
  375.8 7.8 %copy-start.2 = (f32[256,2,2,1024]{3,0,2,1:T(8,128)S(1)}, f32[256,2,2,1024]{3,0,2,1:T(8,128)}, u32[]{:S(2)}) copy-start(f32[256,2,2,1024]{3,0,2,1:T(8,128)} %fusion.34) | copy-start | bytes 12582916
  383.6 5.1 copy-start
  531.0 38.4 %copy-start.4 = (bf16[4,64,3,1024]{3,1,0,2:T(8,128)(2,1)S(1)}, bf16[4,64,3,1024]{3,1,0,2:T(8,128)(2,1)}, u32[]{:S(2)}) copy-start(bf16[4,64,3,1024]{3,1,0,2:T(8,128)(2,1)} %copy-done.3) | copy-start | bytes 4718596
  531.0 38.4 %copy-start.5 = (f32[1024]{0:T(1024)S(1)}, f32[1024]{0:T(1024)}, u32[]{:S(2)}) copy-start(f32[1024]{0:T(1024)} %param.5) | copy-start | bytes 12292
where the time goes:
time: 579 us; the launch traced here: 571 us
  waiting for transfers between devices  252 us (44%)
  blocking collectives  142 us (25%)
  local copies, waits for them, and re-layouts  88 us (15%)
  matrix products  52.7 us (9%)
  starting transfers between devices  25.1 us (4%)
  other arithmetic  10.2 us (2%)
    all_to_all x1, waiting for transfers between devices, body(): lax.all_to_all(jnp.stack([real_part, imag_part]), 'seq', split_axis=2, co...  184 us
    all_to_all x1, blocking collectives, body(): lax.all_to_all(jnp.stack([back_re, back_im]), 'seq', split_axis=2, concat...  105 us
    all_to_all x1, waiting for transfers between devices, body(): lax.all_to_all(stacked_rows.reshape(2, groups, block_len, local_channels)...  51.5 us
    all_to_all x1, blocking collectives, body(): lax.all_to_all(inverted, 'seq', split_axis=0, concat_axis=0, tiled=True)  36.7 us
    all_to_all x1, waiting for transfers between devices, body(): lax.all_to_all(streams, 'ch', split_axis=2, concat_axis=0, tiled=True)  16.2 us
    unnamed x15, local copies, waits for them, and re-layouts  15.7 us
    all_to_all x1, starting transfers between devices, body(): lax.all_to_all(stacked_rows.reshape(2, groups, block_len, local_channels)...  14.4 us
    another operation x1, local copies, waits for them, and re-layouts, body(): jnp.stack([real_part, imag_part])  12.4 us
  transfers between devices with their start and end apart: 3, of which 3 were waited for; matrix products, arithmetic and copies ran while one was open for 1% of the time, Pallas kernels for 0%

commit v1 on v0

v1 whole, which is shorter than its diff:
```python
import functools
import math

import jax
import jax.numpy as jnp
import ml_dtypes
import numpy as np
from jax import lax
from jax.experimental import pallas as pl
from jax.experimental.pallas import tpu as pltpu
from jax.sharding import PartitionSpec as P

MESH = pl.DeviceIdType.MESH
F32 = jnp.float32
BF16 = jnp.bfloat16
R = 128
POWER = 16
TOP = 7.875
FLOOR = 1e-30


def split_np(table):
    high = table.astype(np.float32).astype(ml_dtypes.bfloat16)
    low = (table - high.astype(np.float64)).astype(np.float32).astype(ml_dtypes.bfloat16)
    return high, low


def tables():
    index = np.arange(R, dtype=np.float64)
    theta = (math.pi / 2 + 2 * math.pi * index) / R
    outer = theta[:, None] * index[None, :]
    forward_rows = np.concatenate([np.cos(outer), -np.sin(outer)], 0)
    inverse_rows = np.concatenate([np.cos(outer).T, -np.sin(outer).T], 1)
    twist_re = np.cos(outer / R)
    twist_im = -np.sin(outer / R)
    inner = 2 * math.pi * ((index[:, None] * index[None, :]) % R) / R
    c, s = np.cos(inner), np.sin(inner)
    forward_lanes = np.block([[c, -s], [s, c]])
    inverse_lanes = np.block([[c, s], [-s, c]]) / (R * R)
    mats = []
    for m in (forward_rows, forward_lanes, inverse_lanes, inverse_rows):
        mats.extend(split_np(m))
    twist = np.stack([np.tile(twist_re, (1, 2)), np.tile(twist_im, (1, 2))]).astype(np.float32)
    return mats, twist


def split(x):
    high = x.astype(BF16)
    low = (x - high.astype(F32)).astype(BF16)
    return high, low


def dot(a, b):
    return jnp.dot(a, b, preferred_element_type=F32)


def dot3(a, b):
    return dot(a[0], b[0]) + (dot(a[1], b[0]) + dot(a[0], b[1]))


def scale_of(peak):
    return jnp.log2(jnp.maximum(peak, FLOOR)) - TOP


def encode(x, inverse_scale):
    x = x * inverse_scale
    y = x * x
    y = y * y
    y = y * y
    y = y * y
    return jnp.where(x < 0, -y, y)


def decode(y, log_scale):
    y = y.astype(F32)
    size = jnp.exp2(jnp.log2(jnp.abs(y)) * (1.0 / POWER) + log_scale)
    return jnp.where(y < 0, -size, size)


def kernel(
    streams, taps, skip, f1h, f1l, w2h, w2l, v2h, v2l, i1h, i1l, twist_hbm, out,
    st, hv, gx, gr, qr, qt, sh, rh, eh, reh, sg, rg, eg, reg, so, ro, eo, reo,
    spec, xs, os_, ov, twist, tabs,
    load_sem, gsend, grecv, qsend, qrecv, ssem, rsem,
):
    s = lax.axis_index("seq")
    c = lax.axis_index("ch")
    sz = lax.rem(s, 8)
    sx = lax.rem(s // 8, 2)
    sy = s // 16

    def peer(d):
        y = lax.rem(sy + d // 16, 4)
        x = lax.rem(sx + lax.rem(d // 8, 2), 2)
        z = lax.rem(sz + lax.rem(d, 8), 8)
        return (y * 2 + x) * 8 + z

    barrier = pltpu.get_barrier_semaphore()

    def greet(d, carry):
        pl.semaphore_signal(barrier, inc=1, device_id=(peer(d), c), device_id_type=MESH)
        return carry

    lax.fori_loop(1, 64, greet, 0)
    for d in range(1, 4):
        pl.semaphore_signal(
            barrier, inc=1, device_id=(s, lax.rem(c + d, 4)), device_id_type=MESH
        )

    loads = [
        pltpu.make_async_copy(streams, st, load_sem.at[0]),
        pltpu.make_async_copy(taps, hv, load_sem.at[1]),
        pltpu.make_async_copy(twist_hbm, twist, load_sem.at[2]),
    ]
    for i, source in enumerate((f1h, f1l, w2h, w2l, v2h, v2l, i1h, i1l)):
        loads.append(pltpu.make_async_copy(source, tabs[i], load_sem.at[3 + i]))
    for copy in loads:
        copy.start()

    loads[0].wait()

    def gate(i, carry):
        rows = pl.ds(pl.multiple_of(i * 16, 16), 16)
        gx[rows] = st[1, rows].astype(F32) * st[2, rows].astype(F32)
        return carry

    lax.fori_loop(0, 4, gate, 0)

    def stack_chunks(a, b):
        return jnp.concatenate([a[:, :8], b[:, :8], a[:, 8:], b[:, 8:]], axis=1)

    def encode_group(block, first, send, scales):
        count = block.shape[0] // 16
        block = block.reshape(count, 16, 256)
        a, b = block[:, :, :R], block[:, :, R:]
        peak = jnp.max(jnp.maximum(jnp.abs(a), jnp.abs(b)), axis=1, keepdims=True)
        log_scale = scale_of(peak)
        inverse = jnp.exp2(-log_scale)
        coded = stack_chunks(encode(a, inverse), encode(b, inverse))
        send[pl.ds(first, count)] = coded.astype(BF16)
        scales[pl.ds(first, count)] = log_scale

    loads[1].wait()

    def encode_taps(i, carry):
        encode_group(hv[pl.ds(pl.multiple_of(i * 64, 64), 64), :], i * 4, sh, eh)
        return carry

    lax.fori_loop(0, 16, encode_taps, 0)

    pl.semaphore_wait(barrier, 66)

    mine64 = pl.ds(pl.multiple_of(c * 64, 64), 64)
    copies = []
    for d in (2, 3, 1):
        t = lax.rem(c + d, 4)
        copy = pltpu.make_async_remote_copy(
            gx.at[:, pl.ds(pl.multiple_of(t * 1024, 1024), 1024)],
            gr.at[mine64],
            gsend.at[d - 1],
            grecv.at[d - 1],
            device_id=(s, t),
            device_id_type=MESH,
        )
        copy.start()
        copies.append(copy)

    def send_all(pairs):
        def one(d, carry):
            t = peer(d)
            for source, target, at in pairs:
                pltpu.make_async_remote_copy(
                    source(t), target(s), ssem.at[at], rsem.at[at],
                    device_id=(t, c), device_id_type=MESH,
                ).start()
            return carry

        lax.fori_loop(1, 64, one, 0)

    def whole(ref):
        return lambda i: ref.at[i]

    def half(ref, k):
        return lambda i: ref.at[i, pl.ds(16 * k, 16)]

    def wait_all(ref, sem):
        part = ref.at[pl.ds(0, 63)]
        pltpu.make_async_copy(part, part, sem).wait()

    def wait_half(ref, k, sem):
        part = ref.at[pl.ds(0, 63), pl.ds(16 * k, 16)]
        pltpu.make_async_copy(part, part, sem).wait()

    send_all([(whole(eh), whole(reh), 0), (whole(sh), whole(rh), 1)])
    rh[s] = sh[s]
    reh[s] = eh[s]

    gr[mine64, :] = gx[:, pl.ds(pl.multiple_of(c * 1024, 1024), 1024)]
    for copy in copies:
        copy.wait()

    def encode_gated(j, carry):
        lanes = pl.ds(pl.multiple_of(j * R, R), R)
        encode_group(gr[:, lanes].T, j * 8, sg, eg)
        return carry

    lax.fori_loop(0, 8, encode_gated, 0)

    send_all([(whole(eg), whole(reg), 2), (half(sg, 0), half(rg, 0), 3)])
    send_all([(half(sg, 1), half(rg, 1), 4)])
    rg[s] = sg[s]
    reg[s] = eg[s]

    query_copies = []
    for d in (2, 3, 1):
        t = lax.rem(c + d, 4)
        copy = pltpu.make_async_remote_copy(
            st.at[0, :, pl.ds(pl.multiple_of(t * 1024, 1024), 1024)],
            qr.at[mine64],
            qsend.at[d - 1],
            qrecv.at[d - 1],
            device_id=(s, t),
            device_id_type=MESH,
        )
        copy.start()
        query_copies.append(copy)
    qr[mine64, :] = st[0, :, pl.ds(pl.multiple_of(c * 1024, 1024), 1024)]

    for copy in loads[2:]:
        copy.wait()
    f1 = (tabs[0], tabs[1])
    w2 = (tabs[2], tabs[3])
    v2 = (tabs[4], tabs[5])
    i1 = (tabs[6], tabs[7])

    def get(pair):
        return pair[0][...], pair[1][...]

    def decode_chunk(recv, scales, k):
        def one(i, carry):
            x = decode(recv[pl.ds(i * 4, 4), pl.ds(16 * k, 16)], scales[pl.ds(i * 4, 4)])
            xs[pl.ds(pl.multiple_of(i * 64, 64), 64), :] = x.reshape(64, R)
            return carry

        lax.fori_loop(0, 16, one, 0)

    def forward(p):
        x = jnp.concatenate(
            [xs[pl.ds(2 * p, R, stride=8), :], xs[pl.ds(2 * p + 1, R, stride=8), :]], axis=1
        )
        a = dot3(get(f1), split(x))
        are, aim = a[:R], a[R:]
        tre, tim = twist[0], twist[1]
        bre = are * tre - aim * tim
        bim = are * tim + aim * tre
        rows = jnp.concatenate(
            [
                jnp.concatenate([bre[:, :R], bim[:, :R]], axis=1),
                jnp.concatenate([bre[:, R:], bim[:, R:]], axis=1),
            ],
            axis=0,
        )
        return dot3(split(rows), get(w2))

    wait_all(reh, rsem.at[0])
    wait_all(rh, rsem.at[1])
    for k in range(2):
        decode_chunk(rh, reh, k)

        def transform_taps(p, carry):
            z = forward(p)
            first = s * 16 + 8 * k + 2 * p
            row = lax.broadcasted_iota(jnp.int32, (2 * R, R), 0)
            gain = jnp.where(row < R, skip[first], skip[first + 1])
            spec[k, p] = jnp.concatenate([z[:, :R] + gain, z[:, R:]], axis=1)
            return carry

        lax.fori_loop(0, 4, transform_taps, 0)

    wait_all(reg, rsem.at[2])
    for k in range(2):
        wait_half(rg, k, rsem.at[3 + k])
        decode_chunk(rg, reg, k)

        def convolve(p, carry):
            z = forward(p)
            h = spec[k, p]
            zre, zim, hre, him = z[:, :R], z[:, R:], h[:, :R], h[:, R:]
            prod = jnp.concatenate([zre * hre - zim * him, zre * him + zim * hre], axis=1)
            u = dot3(split(prod), get(v2))
            ure = jnp.concatenate([u[:R, :R], u[R:, :R]], axis=1)
            uim = jnp.concatenate([u[:R, R:], u[R:, R:]], axis=1)
            tre, tim = twist[0], twist[1]
            back = jnp.concatenate([ure * tre + uim * tim, uim * tre - ure * tim], axis=0)
            o = dot3(get(i1), split(back))
            os_[pl.ds(2 * p, R, stride=8), :] = o[:, :R]
            os_[pl.ds(2 * p + 1, R, stride=8), :] = o[:, R:]
            return carry

        lax.fori_loop(0, 4, convolve, 0)

        def encode_result(i, carry):
            x = os_[pl.ds(pl.multiple_of(i * 64, 64), 64), :].reshape(4, 16, R)
            log_scale = scale_of(jnp.max(jnp.abs(x), axis=1, keepdims=True))
            so[k, pl.ds(i * 4, 4)] = encode(x, jnp.exp2(-log_scale)).astype(BF16)
            eo[k, pl.ds(i * 4, 4)] = log_scale
            return carry

        lax.fori_loop(0, 16, encode_result, 0)
        send_all(
            [
                (whole(eo.at[k]), whole(reo.at[k]), 5 + 2 * k),
                (whole(so.at[k]), whole(ro.at[k]), 6 + 2 * k),
            ]
        )
        ro[k, s] = so[k, s]
        reo[k, s] = eo[k, s]
        if k == 0:
            for copy in query_copies:
                copy.wait()

            def turn_queries(j, carry):
                lanes = pl.ds(pl.multiple_of(j * R, R), R)
                rows = pl.ds(pl.multiple_of(j * R, R), R)
                qt[rows, :] = qr[:, lanes].astype(F32).T
                return carry

            lax.fori_loop(0, 8, turn_queries, 0)

    for k in range(2):
        wait_all(reo.at[k], rsem.at[5 + 2 * k])
        wait_all(ro.at[k], rsem.at[6 + 2 * k])

        def finish(i, carry):
            x = decode(ro[k, pl.ds(i * 4, 4)], reo[k, pl.ds(i * 4, 4)])
            x = jnp.concatenate([x[:, :8], x[:, 8:]], axis=2)
            rows = pl.ds(pl.multiple_of(i * 64, 64), 64)
            q = qt[rows, :].reshape(4, 16, 2 * R)
            if k == 0:
                mixed = jnp.concatenate([q[:, :8] * x, q[:, 8:]], axis=1)
                qt[rows, :] = mixed.reshape(64, 2 * R)
            else:
                mixed = jnp.concatenate([q[:, :8], q[:, 8:] * x], axis=1)
                ov[rows, :] = mixed.reshape(64, 2 * R).astype(BF16)
            return carry

        lax.fori_loop(0, 16, finish, 0)

    store = pltpu.make_async_copy(ov, out, load_sem.at[0])
    store.start()
    wait_all(eh, ssem.at[0])
    wait_all(sh, ssem.at[1])
    wait_all(eg, ssem.at[2])
    wait_half(sg, 0, ssem.at[3])
    wait_half(sg, 1, ssem.at[4])
    for k in range(2):
        wait_all(eo.at[k], ssem.at[5 + 2 * k])
        wait_all(so.at[k], ssem.at[6 + 2 * k])
    store.wait()


def body(streams, filter_taps, skip_gain):
    mats, twist = tables()
    streams = jnp.transpose(streams, (1, 0, 2))
    any_spec = pl.BlockSpec(memory_space=pl.ANY)
    dma = pltpu.SemaphoreType.DMA
    vm = pltpu.VMEM
    scratch = [
        vm((3, 64, 4096), BF16),
        vm((1024, 256), F32),
        vm((64, 4096), F32),
        vm((256, 1024), F32),
        vm((256, 1024), BF16),
        vm((1024, 256), F32),
        vm((64, 32, R), BF16),
        vm((64, 32, R), BF16),
        vm((64, 1, R), F32),
        vm((64, 1, R), F32),
        vm((64, 32, R), BF16),
        vm((64, 32, R), BF16),
        vm((64, 1, R), F32),
        vm((64, 1, R), F32),
        vm((2, 64, 16, R), BF16),
        vm((2, 64, 16, R), BF16),
        vm((2, 64, 1, R), F32),
        vm((2, 64, 1, R), F32),
        vm((2, 4, 2 * R, 2 * R), F32),
        vm((1024, R), F32),
        vm((1024, R), F32),
        vm((1024, 256), BF16),
        vm((2, R, 2 * R), F32),
        [vm(m.shape, BF16) for m in mats],
        dma((11,)),
        dma((3,)),
        dma((3,)),
        dma((3,)),
        dma((3,)),
        dma((9,)),
        dma((9,)),
    ]
    return pl.pallas_call(
        kernel,
        out_shape=jax.ShapeDtypeStruct((1024, 256), BF16),
        in_specs=[any_spec, any_spec, pl.BlockSpec(memory_space=pltpu.SMEM)] + [any_spec] * 9,
        out_specs=any_spec,
        scratch_shapes=scratch,
        compiler_params=pltpu.CompilerParams(
            collective_id=0, has_side_effects=True, vmem_limit_bytes=63 * 1024 * 1024
        ),
    )(streams, filter_taps, skip_gain, *[jnp.asarray(m) for m in mats], jnp.asarray(twist))


def solution(mesh):
    placed = (P(("seq", "ch"), None, None), P("ch", "seq"), P("ch"))
    return jax.shard_map(
        body, mesh=mesh, in_specs=placed, out_specs=P("ch", "seq"), check_vma=False
    )
```

time: 579 us -> 74.3 us (0.13)
  the two profiles are of different devices: /device:TPU:32 before, /device:TPU:1 now
where the time goes in v1:
time: 74.3 us; the launch traced here: 74.1 us
  Pallas kernels  72.3 us (97%)
  local copies, waits for them, and re-layouts  1.87 us (3%)
    pallas_call x1, Pallas kernels, body(): pl.pallas_call(kernel, out_shape=jax.ShapeDtypeStruct((1024, 256), BF16),...  72.3 us
    unnamed x1, local copies, waits for them, and re-layouts  1.87 us

profile of v1, /device:TPU:1, one launch (start us, length us, event | category | flops | bytes accessed | tf_op | source)
XLA Modules:
  0.0 74.1 jit_solution(17921587913915319538)
XLA Ops:
  0.0 72.3 %shard_map.118 = bf16[1024,256]{1,0:T(8,128)(2,1)} custom-call(bf16[3,64,4096]{2,1,0:T(8,128)(2,1)} %bitcast.1, f32[1024,256]{1,0:T(8,128)} %taps.1, f32[1024]{0:T(1024)} %skip.1, bf16[256,128]{1,0:T(8,128)(2,1)} %constant.18.clone.f1h, bf16[256,128]{1,0:T(8,128)(2,1)} %constant.19.clone.f1l, bf16[256,256]{1,0:T(8,128)(2,1)} %constant.20.clone.w2h, ...), custom_call_target="tpu_custom_call" | custom-call | tf_op jit(solution)/shard_map/pallas_call | solution.py:401
  72.3 1.9 %copy.14 = bf16[1024,256]{1,0:T(8,128)(2,1)} copy(bf16[1024,256]{1,0:T(8,128)(2,1)} %shard_map.118) | data formatting | bytes 1048576

commit v2 on v1

--- a/solution.py
+++ b/solution.py
@@ -38,9 +38,10 @@
     forward_lanes = np.block([[c, -s], [s, c]])
     inverse_lanes = np.block([[c, s], [-s, c]]) / (R * R)
     mats = []
-    for m in (forward_rows, forward_lanes, inverse_lanes, inverse_rows):
-        mats.extend(split_np(m))
-    twist = np.stack([np.tile(twist_re, (1, 2)), np.tile(twist_im, (1, 2))]).astype(np.float32)
+    for m, axis in ((forward_rows, 1), (forward_lanes, 0), (inverse_lanes, 0), (inverse_rows, 1)):
+        high, low = split_np(m)
+        mats.append(np.concatenate([high, high, low], axis))
+    twist = np.stack([twist_re, twist_im]).astype(np.float32)
     return mats, twist
 
 
@@ -52,10 +53,6 @@
 
 def dot(a, b):
     return jnp.dot(a, b, preferred_element_type=F32)
-
-
-def dot3(a, b):
-    return dot(a[0], b[0]) + (dot(a[1], b[0]) + dot(a[0], b[1]))
 
 
 def scale_of(peak):
@@ -78,10 +75,10 @@
 
 
 def kernel(
-    streams, taps, skip, f1h, f1l, w2h, w2l, v2h, v2l, i1h, i1l, twist_hbm, out,
-    st, hv, gx, gr, qr, qt, sh, rh, eh, reh, sg, rg, eg, reg, so, ro, eo, reo,
-    spec, xs, os_, ov, twist, tabs,
-    load_sem, gsend, grecv, qsend, qrecv, ssem, rsem,
+    streams, taps, skip, f1_hbm, w2_hbm, v2_hbm, i1_hbm, twist_hbm, out,
+    st, hv, gx, gc, gr, ge, gre, qr, qt, sh, rh, eh, reh, sg, rg, eg, reg, so, ro, eo, reo,
+    spec, xs, os_, ov, twist, tabs, wide, first_out, rows3, cols3,
+    load_sem, gsend, grecv, gesend, gerecv, qsend, qrecv, ssem, rsem,
 ):
     s = lax.axis_index("seq")
     c = lax.axis_index("ch")
@@ -112,19 +109,32 @@
         pltpu.make_async_copy(taps, hv, load_sem.at[1]),
         pltpu.make_async_copy(twist_hbm, twist, load_sem.at[2]),
     ]
-    for i, source in enumerate((f1h, f1l, w2h, w2l, v2h, v2l, i1h, i1l)):
+    for i, source in enumerate((f1_hbm, w2_hbm, v2_hbm, i1_hbm)):
         loads.append(pltpu.make_async_copy(source, tabs[i], load_sem.at[3 + i]))
     for copy in loads:
         copy.start()
 
     loads[0].wait()
 
-    def gate(i, carry):
+    def gate(i, peak):
         rows = pl.ds(pl.multiple_of(i * 16, 16), 16)
-        gx[rows] = st[1, rows].astype(F32) * st[2, rows].astype(F32)
+        g = st[1, rows].astype(F32) * st[2, rows].astype(F32)
+        gx[rows] = g
+        g = jnp.abs(g)
+        return jnp.maximum(peak, jnp.max(jnp.maximum(g[:8], g[8:]).reshape(8, 32, R), axis=1))
+
+    peak = lax.fori_loop(0, 4, gate, jnp.zeros((8, R), F32))
+    peak = jnp.max(jnp.max(peak, axis=0, keepdims=True), axis=1, keepdims=True)
+    gate_scale = jnp.ceil(scale_of(jnp.broadcast_to(peak, (1, R))))
+    ge[...] = gate_scale
+    gate_inverse = jnp.exp2(-gate_scale)[:, :1]
+
+    def encode_gate(i, carry):
+        rows = pl.ds(pl.multiple_of(i * 16, 16), 16)
+        gc[rows] = encode(gx[rows], gate_inverse).astype(BF16)
         return carry
 
-    lax.fori_loop(0, 4, gate, 0)
+    lax.fori_loop(0, 4, encode_gate, 0)
 
     def stack_chunks(a, b):
         return jnp.concatenate([a[:, :8], b[:, :8], a[:, 8:], b[:, 8:]], axis=1)
@@ -155,7 +165,17 @@
     for d in (2, 3, 1):
         t = lax.rem(c + d, 4)
         copy = pltpu.make_async_remote_copy(
-            gx.at[:, pl.ds(pl.multiple_of(t * 1024, 1024), 1024)],
+            ge,
+            gre.at[c],
+            gesend.at[d - 1],
+            gerecv.at[d - 1],
+            device_id=(s, t),
+            device_id_type=MESH,
+        )
+        copy.start()
+        copies.append(copy)
+        copy = pltpu.make_async_remote_copy(
+            gc.at[:, pl.ds(pl.multiple_of(t * 1024, 1024), 1024)],
             gr.at[mine64],
             gsend.at[d - 1],
             grecv.at[d - 1],
@@ -191,50 +211,37 @@
         part = ref.at[pl.ds(0, 63), pl.ds(16 * k, 16)]
         pltpu.make_async_copy(part, part, sem).wait()
 
-    send_all([(whole(eh), whole(reh), 0), (whole(sh), whole(rh), 1)])
+    send_all([(whole(eh), whole(reh), 0), (half(sh, 0), half(rh, 0), 1)])
+    send_all([(half(sh, 1), half(rh, 1), 9)])
     rh[s] = sh[s]
     reh[s] = eh[s]
 
-    gr[mine64, :] = gx[:, pl.ds(pl.multiple_of(c * 1024, 1024), 1024)]
+    gr[mine64, :] = gc[:, pl.ds(pl.multiple_of(c * 1024, 1024), 1024)]
+    gre[c] = ge[...]
     for copy in copies:
         copy.wait()
 
+    parts = gre[...]
+    common = jnp.max(parts, axis=0)
+    factor = jnp.exp2((parts - common[None]) * POWER)
+    eg[...] = jnp.broadcast_to(common[None], eg.shape)
+
     def encode_gated(j, carry):
         lanes = pl.ds(pl.multiple_of(j * R, R), R)
-        encode_group(gr[:, lanes].T, j * 8, sg, eg)
+        x = gr[:, lanes].astype(F32).reshape(4, 64, R) * factor
+        x = x.reshape(256, R).T.reshape(8, 16, 256)
+        sg[pl.ds(j * 8, 8)] = stack_chunks(x[:, :, :R], x[:, :, R:]).astype(BF16)
         return carry
 
     lax.fori_loop(0, 8, encode_gated, 0)
 
     send_all([(whole(eg), whole(reg), 2), (half(sg, 0), half(rg, 0), 3)])
-    send_all([(half(sg, 1), half(rg, 1), 4)])
     rg[s] = sg[s]
     reg[s] = eg[s]
 
-    query_copies = []
-    for d in (2, 3, 1):
-        t = lax.rem(c + d, 4)
-        copy = pltpu.make_async_remote_copy(
-            st.at[0, :, pl.ds(pl.multiple_of(t * 1024, 1024), 1024)],
-            qr.at[mine64],
-            qsend.at[d - 1],
-            qrecv.at[d - 1],
-            device_id=(s, t),
-            device_id_type=MESH,
-        )
-        copy.start()
-        query_copies.append(copy)
-    qr[mine64, :] = st[0, :, pl.ds(pl.multiple_of(c * 1024, 1024), 1024)]
-
     for copy in loads[2:]:
         copy.wait()
-    f1 = (tabs[0], tabs[1])
-    w2 = (tabs[2], tabs[3])
-    v2 = (tabs[4], tabs[5])
-    i1 = (tabs[6], tabs[7])
-
-    def get(pair):
-        return pair[0][...], pair[1][...]
+    f1, w2, v2, i1 = tabs
 
     def decode_chunk(recv, scales, k):
         def one(i, carry):
@@ -244,60 +251,87 @@
 
         lax.fori_loop(0, 16, one, 0)
 
-    def forward(p):
-        x = jnp.concatenate(
-            [xs[pl.ds(2 * p, R, stride=8), :], xs[pl.ds(2 * p + 1, R, stride=8), :]], axis=1
-        )
-        a = dot3(get(f1), split(x))
-        are, aim = a[:R], a[R:]
+    def put_rows(at, x):
+        high, low = split(x)
+        rows3[at, 0:256] = high
+        rows3[at, 256:512] = low
+        rows3[at, 512:768] = high
+
+    def forward():
+        x = jnp.concatenate([xs[pl.ds(q, R, stride=8), :] for q in range(8)], axis=1)
+        high, low = split(x)
+        wide[0:R] = high
+        wide[R : 2 * R] = low
+        wide[2 * R : 3 * R] = high
+        first_out[...] = dot(f1[...], wide[...])
         tre, tim = twist[0], twist[1]
-        bre = are * tre - aim * tim
-        bim = are * tim + aim * tre
-        rows = jnp.concatenate(
-            [
-                jnp.concatenate([bre[:, :R], bim[:, :R]], axis=1),
-                jnp.concatenate([bre[:, R:], bim[:, R:]], axis=1),
-            ],
-            axis=0,
-        )
-        return dot3(split(rows), get(w2))
-
-    wait_all(reh, rsem.at[0])
-    wait_all(rh, rsem.at[1])
-    for k in range(2):
-        decode_chunk(rh, reh, k)
-
-        def transform_taps(p, carry):
-            z = forward(p)
+        for q in range(8):
+            lanes = pl.ds(q * R, R)
+            are, aim = first_out[0:R, lanes], first_out[R : 2 * R, lanes]
+            both = jnp.concatenate([are * tre - aim * tim, are * tim + aim * tre], axis=1)
+            put_rows(pl.ds(q * R, R), both)
+
+    def transform_taps(k):
+        forward()
+        for p in range(4):
+            z = dot(rows3[pl.ds(p * 256, 256), :], w2[...])
             first = s * 16 + 8 * k + 2 * p
             row = lax.broadcasted_iota(jnp.int32, (2 * R, R), 0)
             gain = jnp.where(row < R, skip[first], skip[first + 1])
             spec[k, p] = jnp.concatenate([z[:, :R] + gain, z[:, R:]], axis=1)
-            return carry
-
-        lax.fori_loop(0, 4, transform_taps, 0)
+
+    def convolve(k):
+        forward()
+        for p in range(4):
+            rows = pl.ds(p * 256, 256)
+            z = dot(rows3[rows, :], w2[...])
+            h = spec[k, p]
+            zre, zim, hre, him = z[:, :R], z[:, R:], h[:, :R], h[:, R:]
+            put_rows(rows, jnp.concatenate([zre * hre - zim * him, zre * him + zim * hre], axis=1))
+        tre, tim = twist[0], twist[1]
+        for p in range(4):
+            u = dot(rows3[pl.ds(p * 256, 256), :], v2[...])
+            for q in range(2):
+                ure, uim = u[q * R : (q + 1) * R, :R], u[q * R : (q + 1) * R, R:]
+                back = jnp.concatenate([ure * tre + uim * tim, uim * tre - ure * tim], axis=0)
+                high, low = split(back)
+                lanes = pl.ds((2 * p + q) * R, R)
+                cols3[0:256, lanes] = high
+                cols3[256:512, lanes] = low
+                cols3[512:768, lanes] = high
+        o = dot(i1[...], cols3[...])
+        for q in range(8):
+            os_[pl.ds(q, R, stride=8), :] = o[:, q * R : (q + 1) * R]
+
+    wait_all(reh, rsem.at[0])
+    for k in range(2):
+        wait_half(rh, k, rsem.at[1 + 8 * k])
+        decode_chunk(rh, reh, k)
+
+        transform_taps(k)
+        if k == 0:
+            send_all([(half(sg, 1), half(rg, 1), 4)])
+            query_copies = []
+            for d in (2, 3, 1):
+                t = lax.rem(c + d, 4)
+                copy = pltpu.make_async_remote_copy(
+                    st.at[0, :, pl.ds(pl.multiple_of(t * 1024, 1024), 1024)],
+                    qr.at[mine64],
+                    qsend.at[d - 1],
+                    qrecv.at[d - 1],
+                    device_id=(s, t),
+                    device_id_type=MESH,
+                )
+                copy.start()
+                query_copies.append(copy)
+            qr[mine64, :] = st[0, :, pl.ds(pl.multiple_of(c * 1024, 1024), 1024)]
 
     wait_all(reg, rsem.at[2])
     for k in range(2):
         wait_half(rg, k, rsem.at[3 + k])
         decode_chunk(rg, reg, k)
 
-        def convolve(p, carry):
-            z = forward(p)
-            h = spec[k, p]
-            zre, zim, hre, him = z[:, :R], z[:, R:], h[:, :R], h[:, R:]
-            prod = jnp.concatenate([zre * hre - zim * him, zre * him + zim * hre], axis=1)
-            u = dot3(split(prod), get(v2))
-            ure = jnp.concatenate([u[:R, :R], u[R:, :R]], axis=1)
-            uim = jnp.concatenate([u[:R, R:], u[R:, R:]], axis=1)
-            tre, tim = twist[0], twist[1]
-            back = jnp.concatenate([ure * tre + uim * tim, uim * tre - ure * tim], axis=0)
-            o = dot3(get(i1), split(back))
-            os_[pl.ds(2 * p, R, stride=8), :] = o[:, :R]
-            os_[pl.ds(2 * p + 1, R, stride=8), :] = o[:, R:]
-            return carry
-
-        lax.fori_loop(0, 4, convolve, 0)
+        convolve(k)
 
         def encode_result(i, carry):
             x = os_[pl.ds(pl.multiple_of(i * 64, 64), 64), :].reshape(4, 16, R)
@@ -349,7 +383,8 @@
     store = pltpu.make_async_copy(ov, out, load_sem.at[0])
     store.start()
     wait_all(eh, ssem.at[0])
-    wait_all(sh, ssem.at[1])
+    wait_half(sh, 0, ssem.at[1])
+    wait_half(sh, 1, ssem.at[9])
     wait_all(eg, ssem.at[2])
     wait_half(sg, 0, ssem.at[3])
     wait_half(sg, 1, ssem.at[4])
@@ -369,7 +404,10 @@
         vm((3, 64, 4096), BF16),
         vm((1024, 256), F32),
         vm((64, 4096), F32),
-        vm((256, 1024), F32),
+        vm((64, 4096), BF16),
+        vm((256, 1024), BF16),
+        vm((1, R), F32),
+        vm((4, 1, R), F32),
         vm((256, 1024), BF16),
         vm((1024, 256), F32),
         vm((64, 32, R), BF16),
@@ -388,20 +426,26 @@
         vm((1024, R), F32),
         vm((1024, R), F32),
         vm((1024, 256), BF16),
-        vm((2, R, 2 * R), F32),
+        vm((2, R, R), F32),
         [vm(m.shape, BF16) for m in mats],
-        dma((11,)),
-        dma((3,)),
-        dma((3,)),
-        dma((3,)),
-        dma((3,)),
-        dma((9,)),
-        dma((9,)),
+        vm((3 * R, 8 * R), BF16),
+        vm((2 * R, 8 * R), F32),
+        vm((8 * R, 6 * R), BF16),
+        vm((6 * R, 8 * R), BF16),
+        dma((7,)),
+        dma((3,)),
+        dma((3,)),
+        dma((3,)),
+        dma((3,)),
+        dma((3,)),
+        dma((3,)),
+        dma((10,)),
+        dma((10,)),
     ]
     return pl.pallas_call(
         kernel,
         out_shape=jax.ShapeDtypeStruct((1024, 256), BF16),
-        in_specs=[any_spec, any_spec, pl.BlockSpec(memory_space=pltpu.SMEM)] + [any_spec] * 9,
+        in_specs=[any_spec, any_spec, pl.BlockSpec(memory_space=pltpu.SMEM)] + [any_spec] * 5,
         out_specs=any_spec,
         scratch_shapes=scratch,
         compiler_params=pltpu.CompilerParams(

time: 74.3 us -> 63.2 us (0.85)
  Pallas kernels: 72.3 us -> 61.2 us
    pallas_call x1, Pallas kernels: 72.3 us -> 61.2 us  [body(): pl.pallas_call(kernel, out_shape=jax.ShapeDtypeStruct((1024, 256), BF16),...]
where the time goes in v2:
time: 63.2 us; the launch traced here: 63.1 us
  Pallas kernels  61.2 us (97%)
  local copies, waits for them, and re-layouts  1.87 us (3%)
    pallas_call x1, Pallas kernels, body(): pl.pallas_call(kernel, out_shape=jax.ShapeDtypeStruct((1024, 256), BF16),...  61.2 us
    unnamed x1, local copies, waits for them, and re-layouts  1.87 us

profile of v2, /device:TPU:1, one launch (start us, length us, event | category | flops | bytes accessed | tf_op | source)
XLA Modules:
  0.0 63.1 jit_solution(4306263013464151783)
XLA Ops:
  0.0 61.2 %shard_map.82 = bf16[1024,256]{1,0:T(8,128)(2,1)} custom-call(bf16[3,64,4096]{2,1,0:T(8,128)(2,1)} %bitcast.1, f32[1024,256]{1,0:T(8,128)} %taps.1, f32[1024]{0:T(1024)} %skip.1, bf16[256,384]{1,0:T(8,128)(2,1)} %constant.10.clone.f1_hbm, bf16[768,256]{1,0:T(8,128)(2,1)} %constant.11.clone.w2_hbm, bf16[768,256]{1,0:T(8,128)(2,1)} %constant.12.clone.v2_hbm, ...), custom_call_target="tpu_custom_call" | custom-call | tf_op jit(solution)/shard_map/pallas_call | solution.py:445
  61.2 1.9 %copy.10 = bf16[1024,256]{1,0:T(8,128)(2,1)} copy(bf16[1024,256]{1,0:T(8,128)(2,1)} %shard_map.82) | data formatting | bytes 1048576

commit v3 on v2

--- a/solution.py
+++ b/solution.py
@@ -77,8 +77,8 @@
 def kernel(
     streams, taps, skip, f1_hbm, w2_hbm, v2_hbm, i1_hbm, twist_hbm, out,
     st, hv, gx, gc, gr, ge, gre, qr, qt, sh, rh, eh, reh, sg, rg, eg, reg, so, ro, eo, reo,
-    spec, xs, os_, ov, twist, tabs, wide, first_out, rows3, cols3,
-    load_sem, gsend, grecv, gesend, gerecv, qsend, qrecv, ssem, rsem,
+    spec, xs, os_, twist, tabs, wide, first_out, rows3, cols3,
+    load_sem, gsend, grecv, gesend, gerecv, qsend, qrecv, ssem, rsem, scsend, screcv,
 ):
     s = lax.axis_index("seq")
     c = lax.axis_index("ch")
@@ -105,8 +105,8 @@
         )
 
     loads = [
-        pltpu.make_async_copy(streams, st, load_sem.at[0]),
-        pltpu.make_async_copy(taps, hv, load_sem.at[1]),
+        pltpu.make_async_copy(taps, hv, load_sem.at[0]),
+        pltpu.make_async_copy(streams, st, load_sem.at[1]),
         pltpu.make_async_copy(twist_hbm, twist, load_sem.at[2]),
     ]
     for i, source in enumerate((f1_hbm, w2_hbm, v2_hbm, i1_hbm)):
@@ -114,7 +114,31 @@
     for copy in loads:
         copy.start()
 
+    def stack_chunks(a, b):
+        return jnp.concatenate([a[:, :8], b[:, :8], a[:, 8:], b[:, 8:]], axis=1)
+
     loads[0].wait()
+
+    def peak_taps(i, peak):
+        block = jnp.abs(hv[pl.ds(pl.multiple_of(i * 64, 64), 64), :])
+        block = jnp.maximum(block[:, :R], block[:, R:])
+        return jnp.maximum(peak, jnp.max(block.reshape(8, 8, R), axis=0))
+
+    peak = lax.fori_loop(0, 16, peak_taps, jnp.zeros((8, R), F32))
+    tap_scale = scale_of(jnp.max(peak, axis=0, keepdims=True))
+    eh[...] = tap_scale
+    tap_inverse = jnp.exp2(-tap_scale)
+
+    def encode_taps(i, carry):
+        block = hv[pl.ds(pl.multiple_of(i * 64, 64), 64), :]
+        a = encode(block[:, :R], tap_inverse).reshape(4, 16, R)
+        b = encode(block[:, R:], tap_inverse).reshape(4, 16, R)
+        sh[pl.ds(i * 4, 4)] = stack_chunks(a, b).astype(BF16)
+        return carry
+
+    lax.fori_loop(0, 16, encode_taps, 0)
+
+    loads[1].wait()
 
     def gate(i, peak):
         rows = pl.ds(pl.multiple_of(i * 16, 16), 16)
@@ -136,29 +160,59 @@
 
     lax.fori_loop(0, 4, encode_gate, 0)
 
-    def stack_chunks(a, b):
-        return jnp.concatenate([a[:, :8], b[:, :8], a[:, 8:], b[:, 8:]], axis=1)
-
-    def encode_group(block, first, send, scales):
-        count = block.shape[0] // 16
-        block = block.reshape(count, 16, 256)
-        a, b = block[:, :, :R], block[:, :, R:]
-        peak = jnp.max(jnp.maximum(jnp.abs(a), jnp.abs(b)), axis=1, keepdims=True)
-        log_scale = scale_of(peak)
-        inverse = jnp.exp2(-log_scale)
-        coded = stack_chunks(encode(a, inverse), encode(b, inverse))
-        send[pl.ds(first, count)] = coded.astype(BF16)
-        scales[pl.ds(first, count)] = log_scale
-
-    loads[1].wait()
-
-    def encode_taps(i, carry):
-        encode_group(hv[pl.ds(pl.multiple_of(i * 64, 64), 64), :], i * 4, sh, eh)
-        return carry
-
-    lax.fori_loop(0, 16, encode_taps, 0)
-
     pl.semaphore_wait(barrier, 66)
+
+    def send_all(pairs):
+        def one(d, carry):
+            t = peer(d)
+            for source, target, at in pairs:
+                pltpu.make_async_remote_copy(
+                    source(t), target(s), ssem.at[at], rsem.at[at],
+                    device_id=(t, c), device_id_type=MESH,
+                ).start()
+            return carry
+
+        lax.fori_loop(1, 64, one, 0)
+
+    def whole(ref):
+        return lambda i: ref.at[i]
+
+    def half(ref, k):
+        return lambda i: ref.at[i, pl.ds(16 * k, 16)]
+
+    def wait_all(ref, sem):
+        part = ref.at[pl.ds(0, 63)]
+        pltpu.make_async_copy(part, part, sem).wait()
+
+    def wait_half(ref, k, sem):
+        part = ref.at[pl.ds(0, 63), pl.ds(16 * k, 16)]
+        pltpu.make_async_copy(part, part, sem).wait()
+
+    block = s // 8
+    same_block = pl.ds(pl.multiple_of(block * 8, 8), 8)
+
+    def share_lines(row, rows, at):
+        for d in range(1, 8):
+            pltpu.make_async_remote_copy(
+                row, rows.at[s], scsend.at[2 * at], screcv.at[2 * at],
+                device_id=(block * 8 + lax.rem(sz + d, 8), c), device_id_type=MESH,
+            ).start()
+        rows[s] = row[...]
+
+    def wait_rows(rows, count, sem):
+        part = rows.at[pl.ds(0, count)]
+        pltpu.make_async_copy(part, part, sem).wait()
+
+    def share_blocks(rows, at):
+        wait_rows(rows, 7, screcv.at[2 * at])
+        for d in range(1, 8):
+            pltpu.make_async_remote_copy(
+                rows.at[same_block], rows.at[same_block], scsend.at[2 * at + 1], screcv.at[2 * at + 1],
+                device_id=(lax.rem(block + d, 8) * 8 + sz, c), device_id_type=MESH,
+            ).start()
+
+    def wait_scales(rows, at):
+        wait_rows(rows, 56, screcv.at[2 * at + 1])
 
     mine64 = pl.ds(pl.multiple_of(c * 64, 64), 64)
     copies = []
@@ -185,36 +239,10 @@
         copy.start()
         copies.append(copy)
 
-    def send_all(pairs):
-        def one(d, carry):
-            t = peer(d)
-            for source, target, at in pairs:
-                pltpu.make_async_remote_copy(
-                    source(t), target(s), ssem.at[at], rsem.at[at],
-                    device_id=(t, c), device_id_type=MESH,
-                ).start()
-            return carry
-
-        lax.fori_loop(1, 64, one, 0)
-
-    def whole(ref):
-        return lambda i: ref.at[i]
-
-    def half(ref, k):
-        return lambda i: ref.at[i, pl.ds(16 * k, 16)]
-
-    def wait_all(ref, sem):
-        part = ref.at[pl.ds(0, 63)]
-        pltpu.make_async_copy(part, part, sem).wait()
-
-    def wait_half(ref, k, sem):
-        part = ref.at[pl.ds(0, 63), pl.ds(16 * k, 16)]
-        pltpu.make_async_copy(part, part, sem).wait()
-
-    send_all([(whole(eh), whole(reh), 0), (half(sh, 0), half(rh, 0), 1)])
-    send_all([(half(sh, 1), half(rh, 1), 9)])
+    share_lines(eh, reh, 0)
+    send_all([(half(sh, 0), half(rh, 0), 0)])
+    send_all([(half(sh, 1), half(rh, 1), 1)])
     rh[s] = sh[s]
-    reh[s] = eh[s]
 
     gr[mine64, :] = gc[:, pl.ds(pl.multiple_of(c * 1024, 1024), 1024)]
     gre[c] = ge[...]
@@ -224,7 +252,8 @@
     parts = gre[...]
     common = jnp.max(parts, axis=0)
     factor = jnp.exp2((parts - common[None]) * POWER)
-    eg[...] = jnp.broadcast_to(common[None], eg.shape)
+    eg[...] = common
+    share_lines(eg, reg, 1)
 
     def encode_gated(j, carry):
         lanes = pl.ds(pl.multiple_of(j * R, R), R)
@@ -235,9 +264,11 @@
 
     lax.fori_loop(0, 8, encode_gated, 0)
 
-    send_all([(whole(eg), whole(reg), 2), (half(sg, 0), half(rg, 0), 3)])
+    send_all([(half(sg, 0), half(rg, 0), 2)])
+    share_blocks(reh, 0)
+    share_blocks(reg, 1)
+    send_all([(half(sg, 1), half(rg, 1), 3)])
     rg[s] = sg[s]
-    reg[s] = eg[s]
 
     for copy in loads[2:]:
         copy.wait()
@@ -303,14 +334,13 @@
         for q in range(8):
             os_[pl.ds(q, R, stride=8), :] = o[:, q * R : (q + 1) * R]
 
-    wait_all(reh, rsem.at[0])
+    wait_scales(reh, 0)
     for k in range(2):
-        wait_half(rh, k, rsem.at[1 + 8 * k])
+        wait_half(rh, k, rsem.at[k])
         decode_chunk(rh, reh, k)
 
         transform_taps(k)
         if k == 0:
-            send_all([(half(sg, 1), half(rg, 1), 4)])
             query_copies = []
             for d in (2, 3, 1):
                 t = lax.rem(c + d, 4)
@@ -326,29 +356,31 @@
                 query_copies.append(copy)
             qr[mine64, :] = st[0, :, pl.ds(pl.multiple_of(c * 1024, 1024), 1024)]
 
-    wait_all(reg, rsem.at[2])
+    wait_scales(reg, 1)
     for k in range(2):
-        wait_half(rg, k, rsem.at[3 + k])
+        wait_half(rg, k, rsem.at[2 + k])
         decode_chunk(rg, reg, k)
 
         convolve(k)
 
+        def peak_result(i, peak):
+            x = jnp.abs(os_[pl.ds(pl.multiple_of(i * 64, 64), 64), :])
+            return jnp.maximum(peak, jnp.max(x.reshape(8, 8, R), axis=0))
+
+        peak = lax.fori_loop(0, 16, peak_result, jnp.zeros((8, R), F32))
+        log_scale = scale_of(jnp.max(peak, axis=0, keepdims=True))
+        eo[k] = log_scale
+        share_lines(eo.at[k], reo.at[k], 2 + k)
+        inverse = jnp.exp2(-log_scale)
+
         def encode_result(i, carry):
-            x = os_[pl.ds(pl.multiple_of(i * 64, 64), 64), :].reshape(4, 16, R)
-            log_scale = scale_of(jnp.max(jnp.abs(x), axis=1, keepdims=True))
-            so[k, pl.ds(i * 4, 4)] = encode(x, jnp.exp2(-log_scale)).astype(BF16)
-            eo[k, pl.ds(i * 4, 4)] = log_scale
+            x = encode(os_[pl.ds(pl.multiple_of(i * 64, 64), 64), :], inverse)
+            so[k, pl.ds(i * 4, 4)] = x.reshape(4, 16, R).astype(BF16)
             return carry
 
         lax.fori_loop(0, 16, encode_result, 0)
-        send_all(
-            [
-                (whole(eo.at[k]), whole(reo.at[k]), 5 + 2 * k),
-                (whole(so.at[k]), whole(ro.at[k]), 6 + 2 * k),
-            ]
-        )
+        send_all([(whole(so.at[k]), whole(ro.at[k]), 4 + k)])
         ro[k, s] = so[k, s]
-        reo[k, s] = eo[k, s]
         if k == 0:
             for copy in query_copies:
                 copy.wait()
@@ -360,10 +392,12 @@
                 return carry
 
             lax.fori_loop(0, 8, turn_queries, 0)
-
+            share_blocks(reo.at[0], 2)
+
+    share_blocks(reo.at[1], 3)
     for k in range(2):
-        wait_all(reo.at[k], rsem.at[5 + 2 * k])
-        wait_all(ro.at[k], rsem.at[6 + 2 * k])
+        wait_scales(reo.at[k], 2 + k)
+        wait_all(ro.at[k], rsem.at[4 + k])
 
         def finish(i, carry):
             x = decode(ro[k, pl.ds(i * 4, 4)], reo[k, pl.ds(i * 4, 4)])
@@ -375,29 +409,24 @@
                 qt[rows, :] = mixed.reshape(64, 2 * R)
             else:
                 mixed = jnp.concatenate([q[:, :8], q[:, 8:] * x], axis=1)
-                ov[rows, :] = mixed.reshape(64, 2 * R).astype(BF16)
+                out[rows, :] = mixed.reshape(64, 2 * R).astype(BF16)
             return carry
 
         lax.fori_loop(0, 16, finish, 0)
 
-    store = pltpu.make_async_copy(ov, out, load_sem.at[0])
-    store.start()
-    wait_all(eh, ssem.at[0])
-    wait_half(sh, 0, ssem.at[1])
-    wait_half(sh, 1, ssem.at[9])
-    wait_all(eg, ssem.at[2])
-    wait_half(sg, 0, ssem.at[3])
-    wait_half(sg, 1, ssem.at[4])
     for k in range(2):
-        wait_all(eo.at[k], ssem.at[5 + 2 * k])
-        wait_all(so.at[k], ssem.at[6 + 2 * k])
-    store.wait()
+        wait_half(sh, k, ssem.at[k])
+        wait_half(sg, k, ssem.at[2 + k])
+        wait_all(so.at[k], ssem.at[4 + k])
+    for i, rows in enumerate((reh, reg, reo.at[0], reo.at[1])):
+        wait_rows(rows, 7, scsend.at[2 * i])
+        wait_rows(rows, 56, scsend.at[2 * i + 1])
 
 
 def body(streams, filter_taps, skip_gain):
     mats, twist = tables()
     streams = jnp.transpose(streams, (1, 0, 2))
-    any_spec = pl.BlockSpec(memory_space=pl.ANY)
+    any_spec = pl.BlockSpec(memory_space=pltpu.HBM)
     dma = pltpu.SemaphoreType.DMA
     vm = pltpu.VMEM
     scratch = [
@@ -412,20 +441,19 @@
         vm((1024, 256), F32),
         vm((64, 32, R), BF16),
         vm((64, 32, R), BF16),
-        vm((64, 1, R), F32),
+        vm((1, R), F32),
         vm((64, 1, R), F32),
         vm((64, 32, R), BF16),
         vm((64, 32, R), BF16),
-        vm((64, 1, R), F32),
+        vm((1, R), F32),
         vm((64, 1, R), F32),
         vm((2, 64, 16, R), BF16),
         vm((2, 64, 16, R), BF16),
-        vm((2, 64, 1, R), F32),
+        vm((2, 1, R), F32),
         vm((2, 64, 1, R), F32),
         vm((2, 4, 2 * R, 2 * R), F32),
         vm((1024, R), F32),
         vm((1024, R), F32),
-        vm((1024, 256), BF16),
         vm((2, R, R), F32),
         [vm(m.shape, BF16) for m in mats],
         vm((3 * R, 8 * R), BF16),
@@ -439,14 +467,16 @@
         dma((3,)),
         dma((3,)),
         dma((3,)),
-        dma((10,)),
-        dma((10,)),
+        dma((6,)),
+        dma((6,)),
+        dma((8,)),
+        dma((8,)),
     ]
     return pl.pallas_call(
         kernel,
-        out_shape=jax.ShapeDtypeStruct((1024, 256), BF16),
+        out_shape=pltpu.VMEM((1024, 256), BF16),
         in_specs=[any_spec, any_spec, pl.BlockSpec(memory_space=pltpu.SMEM)] + [any_spec] * 5,
-        out_specs=any_spec,
+        out_specs=pl.BlockSpec(memory_space=pltpu.VMEM),
         scratch_shapes=scratch,
         compiler_params=pltpu.CompilerParams(
             collective_id=0, has_side_effects=True, vmem_limit_bytes=63 * 1024 * 1024

time: 63.2 us -> 58.5 us (0.926)
  Pallas kernels: 61.2 us -> 57.3 us
  local copies, waits for them, and re-layouts: 1.87 us -> 0.8 us
    pallas_call x1, Pallas kernels: 61.2 us -> 57.3 us  [body(): pl.pallas_call(kernel, out_shape=pltpu.VMEM((1024, 256), BF16), in_specs=...]
    unnamed x1, local copies, waits for them, and re-layouts: 1.87 us -> 0.8 us
where the time goes in v3:
time: 58.5 us; the launch traced here: 58.1 us
  Pallas kernels  57.3 us (98%)
  local copies, waits for them, and re-layouts  0.8 us (1%)
    pallas_call x1, Pallas kernels, body(): pl.pallas_call(kernel, out_shape=pltpu.VMEM((1024, 256), BF16), in_specs=...  57.3 us

profile of v3, /device:TPU:1, one launch (start us, length us, event | category | flops | bytes accessed | tf_op | source)
XLA Modules:
  0.0 58.1 jit_solution(11725745983688127299)
XLA Ops:
  0.0 57.3 %shard_map.82 = bf16[1024,256]{1,0:T(8,128)(2,1)S(1)} custom-call(bf16[3,64,4096]{2,1,0:T(8,128)(2,1)} %bitcast.1, f32[1024,256]{1,0:T(8,128)} %taps.1, f32[1024]{0:T(1024)} %skip.1, bf16[256,384]{1,0:T(8,128)(2,1)} %constant.10.clone.f1_hbm, bf16[768,256]{1,0:T(8,128)(2,1)} %constant.11.clone.w2_hbm, bf16[768,256]{1,0:T(8,128)(2,1)} %constant.12.clone.v2_hbm, ...), custom_call_target="tpu_custom_call" | custom-call | tf_op jit(solution)/shard_map/pallas_call | solution.py:475
  57.3 0.8 %copy.10 = bf16[1024,256]{1,0:T(8,128)(2,1)} copy(bf16[1024,256]{1,0:T(8,128)(2,1)S(1)} %shard_map.82) | data formatting | bytes 1048576

commit v4 on v3

--- a/solution.py
+++ b/solution.py
@@ -382,18 +382,18 @@
         send_all([(whole(so.at[k]), whole(ro.at[k]), 4 + k)])
         ro[k, s] = so[k, s]
         if k == 0:
-            for copy in query_copies:
-                copy.wait()
-
-            def turn_queries(j, carry):
-                lanes = pl.ds(pl.multiple_of(j * R, R), R)
-                rows = pl.ds(pl.multiple_of(j * R, R), R)
-                qt[rows, :] = qr[:, lanes].astype(F32).T
-                return carry
-
-            lax.fori_loop(0, 8, turn_queries, 0)
             share_blocks(reo.at[0], 2)
 
+    for copy in query_copies:
+        copy.wait()
+
+    def turn_queries(j, carry):
+        lanes = pl.ds(pl.multiple_of(j * R, R), R)
+        rows = pl.ds(pl.multiple_of(j * R, R), R)
+        qt[rows, :] = qr[:, lanes].astype(F32).T
+        return carry
+
+    lax.fori_loop(0, 8, turn_queries, 0)
     share_blocks(reo.at[1], 3)
     for k in range(2):
         wait_scales(reo.at[k], 2 + k)
@@ -452,8 +452,8 @@
         vm((2, 1, R), F32),
         vm((2, 64, 1, R), F32),
         vm((2, 4, 2 * R, 2 * R), F32),
-        vm((1024, R), F32),
-        vm((1024, R), F32),
+        vm((1032, R), F32),
+        vm((1032, R), F32),
         vm((2, R, R), F32),
         [vm(m.shape, BF16) for m in mats],
         vm((3 * R, 8 * R), BF16),

time: 58.5 us -> 58.1 us (level)
  no operation moved by 1% of the time
where the time goes in v4:
time: 58.1 us; the launch traced here: 58 us
  Pallas kernels  57.2 us (98%)
  local copies, waits for them, and re-layouts  0.8 us (1%)
    pallas_call x1, Pallas kernels, body(): pl.pallas_call(kernel, out_shape=pltpu.VMEM((1024, 256), BF16), in_specs=...  57.2 us

profile of v4, /device:TPU:1, one launch (start us, length us, event | category | flops | bytes accessed | tf_op | source)
XLA Modules:
  0.0 58.0 jit_solution(10263272762010839240)
XLA Ops:
  0.0 57.2 %shard_map.82 = bf16[1024,256]{1,0:T(8,128)(2,1)S(1)} custom-call(bf16[3,64,4096]{2,1,0:T(8,128)(2,1)} %bitcast.1, f32[1024,256]{1,0:T(8,128)} %taps.1, f32[1024]{0:T(1024)} %skip.1, bf16[256,384]{1,0:T(8,128)(2,1)} %constant.10.clone.f1_hbm, bf16[768,256]{1,0:T(8,128)(2,1)} %constant.11.clone.w2_hbm, bf16[768,256]{1,0:T(8,128)(2,1)} %constant.12.clone.v2_hbm, ...), custom_call_target="tpu_custom_call" | custom-call | tf_op jit(solution)/shard_map/pallas_call | solution.py:475
  57.2 0.8 %copy.10 = bf16[1024,256]{1,0:T(8,128)(2,1)} copy(bf16[1024,256]{1,0:T(8,128)(2,1)S(1)} %shard_map.82) | data formatting | bytes 1048576

commit v5 on v4

--- a/solution.py
+++ b/solution.py
@@ -262,7 +262,7 @@
         sg[pl.ds(j * 8, 8)] = stack_chunks(x[:, :, :R], x[:, :, R:]).astype(BF16)
         return carry
 
-    lax.fori_loop(0, 8, encode_gated, 0)
+    lax.fori_loop(0, 8, encode_gated, 0, unroll=2)
 
     send_all([(half(sg, 0), half(rg, 0), 2)])
     share_blocks(reh, 0)
@@ -280,7 +280,7 @@
             xs[pl.ds(pl.multiple_of(i * 64, 64), 64), :] = x.reshape(64, R)
             return carry
 
-        lax.fori_loop(0, 16, one, 0)
+        lax.fori_loop(0, 16, one, 0, unroll=2)
 
     def put_rows(at, x):
         high, low = split(x)
@@ -378,7 +378,7 @@
             so[k, pl.ds(i * 4, 4)] = x.reshape(4, 16, R).astype(BF16)
             return carry
 
-        lax.fori_loop(0, 16, encode_result, 0)
+        lax.fori_loop(0, 16, encode_result, 0, unroll=2)
         send_all([(whole(so.at[k]), whole(ro.at[k]), 4 + k)])
         ro[k, s] = so[k, s]
         if k == 0:

time: 58.1 us -> 57.8 us (level)
  no operation moved by 1% of the time
where the time goes in v5:
time: 57.8 us; the launch traced here: 57.7 us
  Pallas kernels  56.9 us (98%)
  local copies, waits for them, and re-layouts  0.8 us (1%)
    pallas_call x1, Pallas kernels, body(): pl.pallas_call(kernel, out_shape=pltpu.VMEM((1024, 256), BF16), in_specs=...  56.9 us

profile of v5, /device:TPU:1, one launch (start us, length us, event | category | flops | bytes accessed | tf_op | source)
XLA Modules:
  0.0 57.7 jit_solution(12292345820121270519)
XLA Ops:
  0.0 56.9 %shard_map.82 = bf16[1024,256]{1,0:T(8,128)(2,1)S(1)} custom-call(bf16[3,64,4096]{2,1,0:T(8,128)(2,1)} %bitcast.1, f32[1024,256]{1,0:T(8,128)} %taps.1, f32[1024]{0:T(1024)} %skip.1, bf16[256,384]{1,0:T(8,128)(2,1)} %constant.10.clone.f1_hbm, bf16[768,256]{1,0:T(8,128)(2,1)} %constant.11.clone.w2_hbm, bf16[768,256]{1,0:T(8,128)(2,1)} %constant.12.clone.v2_hbm, ...), custom_call_target="tpu_custom_call" | custom-call | tf_op jit(solution)/shard_map/pallas_call | solution.py:475
  56.9 0.8 %copy.10 = bf16[1024,256]{1,0:T(8,128)(2,1)} copy(bf16[1024,256]{1,0:T(8,128)(2,1)S(1)} %shard_map.82) | data formatting | bytes 1048576
